TPU v7x, 32 devices: a whole 2x2x4 slice. The times are simulated.
32 devices in a mesh: seq: 8 (over y, x, core), chan: 4 (over z).
Axes of the slice: x: 2, y: 2, z: 4, core: 2. Of those that a mesh axis runs over, the one named last changes fastest.
Arguments:
- features: bfloat16 [3, 2, 8192, 1024], P(None, None, 'chan', 'seq'), may hold values from -6 to 6
- offsets: int32 [2], replicated, may hold values from 0 to 511
- tokens: int32 [2, 4], replicated, may hold values from 0 to 511
- decay_rate: float32 [16, 8192], P(None, 'chan'), may hold values from 0 to 1
- residue: float32 [16, 8192], P(None, 'chan'), may hold values from -1 to 1
- skip_weight: float32 [8192], P('chan'), may hold values from -3 to 3
- embedding: bfloat16 [512, 8192], P(None, 'seq'), may hold values from -12 to 12
- norm_gain: float32 [8192], P('seq'), may hold values from 0.1 to 1.9
- dec_weight: bfloat16 [3, 8192, 8192], P(None, 'seq', 'chan'), may hold values from -0.09375 to 0.09375
- out_weight: bfloat16 [8192, 8192], P('chan', 'seq'), may hold values from -0.09375 to 0.09375
Outputs:
- mixed: bfloat16 [2, 8192, 1024], P(None, 'chan', 'seq')
- decoded: bfloat16 [2, 4, 8192], P(None, None, ('seq', 'chan'))
All inputs are finite; a program needn't handle non-finite values.
Results may differ from a plain program's by a relative error of at most 0.0082.
Values may be sent and summed in bfloat16 or wider, within the bound.
A program may use at most 128 MiB of HBM per device.

v0:
```python
import math

import jax
import jax.numpy as jnp
from jax import lax
from jax.sharding import PartitionSpec as P

D = 8192


highest = lax.Precision.HIGHEST


def carried_in(value, axis, join, neutral):
    count, mine = (lax.axis_size(axis), lax.axis_index(axis))
    pieces = jax.tree.map(lambda part: lax.all_gather(part, axis), value)
    subtotal = jax.tree.map(
        lambda part, zero: jnp.full_like(part, 0) + jnp.asarray(zero, part.dtype), value, neutral
    )

    def hop(position, subtotal):
        longer = join(subtotal, jax.tree.map(lambda part: part[position], pieces))
        return jax.tree.map(lambda new, old: jnp.where(position < mine, new, old), longer, subtotal)

    return lax.fori_loop(0, count - 1, hop, subtotal)


def local_conv(signal, rates, residues, skips, start_state):
    batch_rows, channels, length = signal.shape
    modes = rates.shape[0]
    block = math.gcd(length, 256)
    blocks = length // block
    group = math.gcd(channels, max(1, 2**21 // (block * block)))
    groups = channels // group

    def one_group(packed):
        sig_group, rate_group, res_group, skip_group, start_group = packed
        expo = -rate_group
        lag_pos = jnp.arange(block, dtype=jnp.float32)
        filt = jnp.sum(res_group[:, :, None] * jnp.exp(expo[:, :, None] * lag_pos), axis=0)
        distance = jnp.arange(block)[:, None] - jnp.arange(block)[None, :]
        toeplitz = jnp.where(distance >= 0, jnp.take(filt, jnp.maximum(distance, 0), axis=1), 0.0)
        blocked = sig_group.reshape(batch_rows, group, blocks, block)
        inner = jnp.einsum("gij,bgnj->bgni", toeplitz, blocked, precision=highest)
        tail_weight = jnp.exp(expo[:, :, None] * (block - 1.0 - lag_pos))
        block_sums = jnp.einsum("mgj,bgnj->bmgn", tail_weight, blocked, precision=highest)
        block_pos = jnp.arange(blocks, dtype=jnp.float32)
        block_gap = block_pos[:, None] - 1.0 - block_pos[None, :]
        spread = jnp.where(
            block_gap >= 0,
            jnp.exp(expo[:, :, None, None] * block * jnp.maximum(block_gap, 0.0)),
            0.0,
        )
        carried = jnp.einsum("mgnk,bmgk->bmgn", spread, block_sums, precision=highest)
        carried = (
            carried + jnp.exp(expo[:, :, None] * block * block_pos)[None] * start_group[..., None]
        )
        head_weight = res_group[:, :, None] * jnp.exp(expo[:, :, None] * (lag_pos + 1.0))
        outer = jnp.einsum("mgi,bmgn->bgni", head_weight, carried, precision=highest)
        conv = (inner + outer).reshape(batch_rows, group, length) + skip_group[
            None, :, None
        ] * sig_group
        final = jnp.exp(expo * block)[None] * carried[..., -1] + block_sums[..., -1]
        return (conv, final)

    packed = (
        signal.reshape(batch_rows, groups, group, length).transpose(1, 0, 2, 3),
        rates.reshape(modes, groups, group).transpose(1, 0, 2),
        residues.reshape(modes, groups, group).transpose(1, 0, 2),
        skips.reshape(groups, group),
        start_state.reshape(batch_rows, modes, groups, group).transpose(2, 0, 1, 3),
    )
    conv, final = lax.map(one_group, packed)
    conv = conv.transpose(1, 0, 2, 3).reshape(batch_rows, channels, length)
    final = final.transpose(1, 2, 0, 3).reshape(batch_rows, modes, channels)
    return (conv, final)


def body(
    features,
    offsets,
    tokens,
    decay_rate,
    residue,
    skip_weight,
    embedding,
    norm_gain,
    dec_weight,
    out_weight,
):
    seq_count = lax.axis_size("seq")
    seq_index = lax.axis_index("seq")
    query = features[0]
    keys_in = features[1]
    values_in = features[2]
    batch_rows, local_chans, shard_len = query.shape
    positions = seq_index * shard_len + jnp.arange(shard_len, dtype=jnp.int32)
    live = positions[None, :] >= offsets[:, None]
    product = jnp.where(
        live[:, None, :], keys_in.astype(jnp.float32) * values_in.astype(jnp.float32), 0.0
    ).astype(jnp.bfloat16)
    per_device = local_chans // seq_count
    own_rates = lax.dynamic_slice_in_dim(decay_rate, seq_index * per_device, per_device, 1)
    own_residue = lax.dynamic_slice_in_dim(residue, seq_index * per_device, per_device, 1)
    own_skip = lax.dynamic_slice_in_dim(skip_weight, seq_index * per_device, per_device, 0)
    signal = product.astype(jnp.float32)
    lag_pos = jnp.arange(shard_len, dtype=jnp.float32)
    weights = jnp.exp(-decay_rate[:, :, None] * (shard_len - 1.0 - lag_pos))
    shard_ends = jnp.einsum("mcj,bcj->bmc", weights, signal, precision=highest)
    power = jnp.exp(-decay_rate * shard_len)

    def combine(earlier, later):
        return (earlier[0] * later[0], later[1] + later[0][None] * earlier[1])

    prefix = carried_in(
        (power, shard_ends), "seq", combine, (jnp.ones_like(power), jnp.zeros_like(shard_ends))
    )
    conv, unused = local_conv(signal, decay_rate, residue, skip_weight, prefix[1])
    mixed = (query.astype(jnp.float32) * conv).astype(jnp.bfloat16)
    later_len = ((seq_count - 1 - seq_index) * shard_len).astype(jnp.float32)
    weighted = shard_ends * jnp.exp(-decay_rate * later_len)[None]
    state = lax.psum_scatter(weighted, "seq", scatter_dimension=2, tiled=True)
    steps = tokens.shape[1]
    vocab = embedding.shape[0]
    flat_tokens = tokens.reshape(-1)
    one_hot = (flat_tokens[:, None] == jnp.arange(vocab, dtype=jnp.int32)[None, :]).astype(
        jnp.bfloat16
    )
    embedded = jnp.dot(one_hot, embedding, preferred_element_type=jnp.float32)
    partial_sq = jnp.sum(embedded * embedded, axis=1)
    total_sq = lax.psum(partial_sq, "seq")
    normed = (embedded * lax.rsqrt(total_sq / D + 1e-05)[:, None] * norm_gain[None, :]).astype(
        jnp.bfloat16
    )
    proj_terms = jnp.einsum("td,idc->itc", normed, dec_weight, preferred_element_type=jnp.float32)
    projected = lax.psum_scatter(proj_terms, "seq", scatter_dimension=2, tiled=True).astype(
        jnp.bfloat16
    )
    projected = projected.reshape(3, batch_rows, steps, per_device)
    decay = jnp.exp(-own_rates)
    running = state
    outputs = []
    for step in range(steps):
        rounded = lax.optimization_barrier(
            (
                projected[1, :, step].astype(jnp.float32)
                * projected[2, :, step].astype(jnp.float32)
            ).astype(jnp.bfloat16)
        )
        mixed_in = rounded.astype(jnp.float32)
        running = decay[None] * running + mixed_in[:, None, :]
        conv_step = jnp.sum(own_residue[None] * running, axis=1) + own_skip[None] * mixed_in
        outputs.append((projected[0, :, step].astype(jnp.float32) * conv_step).astype(jnp.bfloat16))
    decode_mix = jnp.stack(outputs, axis=1)
    piece = lax.all_gather(decode_mix, "seq", axis=2, tiled=True)
    piece_width = piece.shape[2]
    summed = jnp.dot(piece.reshape(-1, piece_width), out_weight, preferred_element_type=jnp.float32)
    decoded = lax.psum_scatter(summed, "chan", scatter_dimension=1, tiled=True).astype(jnp.bfloat16)
    decoded = decoded.reshape(batch_rows, steps, -1)
    return (mixed, decoded)


def solution(mesh):
    placed = (
        P(None, None, "chan", "seq"),
        P(),
        P(),
        P(None, "chan"),
        P(None, "chan"),
        P("chan"),
        P(None, "seq"),
        P("seq"),
        P(None, "seq", "chan"),
        P("chan", "seq"),
    )
    return jax.shard_map(
        body,
        mesh=mesh,
        in_specs=placed,
        out_specs=(P(None, "chan", "seq"), P(None, None, ("seq", "chan"))),
        check_vma=False,
    )
```

profile of v0, /device:TPU:0, one launch (start us, length us, event | category | flops | bytes accessed | tf_op | source)
XLA Modules:
  0.0 1663.5 jit_solution(5821602378818590767)
XLA Ops:
  14.1 28.1 %broadcast_multiply_fusion = (f32[2,16,2048]{1,0,2:T(2,128)}, f32[2,16,2048]{1,0,2:T(2,128)S(1)}) fusion(f32[16,2048]{0,1:T(8,128)S(1)} %copy-done.2, f32[128]{0:T(128)S(1)} %iota_subtract_fusion.2, f32[16,2048]{0,1:T(8,128)S(1)} %copy-done.1, bf16[2,2048,128]{2,1,0:T(8,128)(2,1)S(1)} %fusion.41), kind=kOutput, calls=%fused_computation.66 | convolution fusion | flops 104923136 | bytes 1835520 | tf_op jit(solution)/shard_map/mcj,bcj->bmc/dot_general | solution.py:109
  70.0 36.8 %all-reduce.3.cloned.1.call-done = f32[2,16,2048]{1,0,2:T(2,128)} async-done(((f32[2,16,2048]{1,0,2:T(2,128)}), f32[2,16,2048]{1,0,2:T(2,128)}) %all-reduce.3.cloned.1.call-update) | async-done | bytes 262160
  108.5 34.6 %reduce-scatter.3.cloned.1.call-done = f32[3,8,256]{2,1,0:T(8,128)} async-done(((f32[3,8,2048]{2,1,0:T(8,128)}), f32[3,8,256]{2,1,0:T(8,128)}) %reduce-scatter.3.cloned.1.call-update) | async-done | bytes 24592 | tf_op jit(solution)/shard_map/reduce_scatter | solution.py:136
  178.3 22.2 %all-gather.7.cloned.1.call-done = f32[128,2048]{1,0:T(8,128)} async-done(((f32[16,2048]{1,0:T(8,128)}), f32[128,2048]{1,0:T(8,128)}) %all-gather.7.cloned.1.call-update) | async-done | bytes 1048592 | tf_op jit(solution)/shard_map/all_gather | solution.py:16
  200.5 29.7 %all-gather.5.cloned.1.call-done = f32[16,16,2048]{2,1,0:T(8,128)} async-done(((f32[2,16,2048]{2,1,0:T(8,128)}), f32[16,16,2048]{2,1,0:T(8,128)}) %all-gather.5.cloned.1.call-update) | async-done | bytes 2097168 | tf_op jit(solution)/shard_map/all_gather | solution.py:16
  246.6 1406.0 %while.27 = (s32[]{:T(128)}, f32[16,2,128,128]{3,1,2,0:T(2,128)}, f32[16,2,128,128]{3,1,2,0:T(2,128)S(1)}, f32[16,16,128]{1,2,0:T(8,128)}, f32[16,16,128]{1,2,0:...) while((s32[]{:T(128)}, f32[16,2,128,128]{3,1,2,0:T(2,128)}, ...), condition=%wide.region_4.5_spmd, body=%wide.region_2.4_spmd.sunk | while | flops 68894976 | bytes 43496548 | solution.py:73
  249.0 54.8 %gather_fusion = f32[16384,128]{1,0:T(8,128)} fusion(f32[128,128]{0,1:T(8,128)S(1)} %copy.265, s32[16384]{0:T(1024)S(1)} %bitcast_clamp_fusion.2), kind=kCustom, calls=%fused_computation.clone.1 | custom fusion | bytes 16842752 | tf_op jit(solution)/shard_map/while/body/eval_jaxpr/jit(_take)/gather | solution.py:42
  313.2 15.4 fusion.88
  336.9 54.8 %gather_fusion = f32[16384,128]{1,0:T(8,128)} fusion(f32[128,128]{0,1:T(8,128)S(1)} %copy.265, s32[16384]{0:T(1024)S(1)} %bitcast_clamp_fusion.2), kind=kCustom, calls=%fused_computation.clone.1 | custom fusion | bytes 16842752 | tf_op jit(solution)/shard_map/while/body/eval_jaxpr/jit(_take)/gather | solution.py:42
  401.1 15.4 fusion.88
  424.8 54.8 %gather_fusion = f32[16384,128]{1,0:T(8,128)} fusion(f32[128,128]{0,1:T(8,128)S(1)} %copy.265, s32[16384]{0:T(1024)S(1)} %bitcast_clamp_fusion.2), kind=kCustom, calls=%fused_computation.clone.1 | custom fusion | bytes 16842752 | tf_op jit(solution)/shard_map/while/body/eval_jaxpr/jit(_take)/gather | solution.py:42
  512.6 54.8 %gather_fusion = f32[16384,128]{1,0:T(8,128)} fusion(f32[128,128]{0,1:T(8,128)S(1)} %copy.265, s32[16384]{0:T(1024)S(1)} %bitcast_clamp_fusion.2), kind=kCustom, calls=%fused_computation.clone.1 | custom fusion | bytes 16842752 | tf_op jit(solution)/shard_map/while/body/eval_jaxpr/jit(_take)/gather | solution.py:42
  600.5 54.8 %gather_fusion = f32[16384,128]{1,0:T(8,128)} fusion(f32[128,128]{0,1:T(8,128)S(1)} %copy.265, s32[16384]{0:T(1024)S(1)} %bitcast_clamp_fusion.2), kind=kCustom, calls=%fused_computation.clone.1 | custom fusion | bytes 16842752 | tf_op jit(solution)/shard_map/while/body/eval_jaxpr/jit(_take)/gather | solution.py:42
  688.4 54.8 %gather_fusion = f32[16384,128]{1,0:T(8,128)} fusion(f32[128,128]{0,1:T(8,128)S(1)} %copy.265, s32[16384]{0:T(1024)S(1)} %bitcast_clamp_fusion.2), kind=kCustom, calls=%fused_computation.clone.1 | custom fusion | bytes 16842752 | tf_op jit(solution)/shard_map/while/body/eval_jaxpr/jit(_take)/gather | solution.py:42
  776.3 54.8 %gather_fusion = f32[16384,128]{1,0:T(8,128)} fusion(f32[128,128]{0,1:T(8,128)S(1)} %copy.265, s32[16384]{0:T(1024)S(1)} %bitcast_clamp_fusion.2), kind=kCustom, calls=%fused_computation.clone.1 | custom fusion | bytes 16842752 | tf_op jit(solution)/shard_map/while/body/eval_jaxpr/jit(_take)/gather | solution.py:42
  864.1 54.8 %gather_fusion = f32[16384,128]{1,0:T(8,128)} fusion(f32[128,128]{0,1:T(8,128)S(1)} %copy.265, s32[16384]{0:T(1024)S(1)} %bitcast_clamp_fusion.2), kind=kCustom, calls=%fused_computation.clone.1 | custom fusion | bytes 16842752 | tf_op jit(solution)/shard_map/while/body/eval_jaxpr/jit(_take)/gather | solution.py:42
  952.0 54.8 %gather_fusion = f32[16384,128]{1,0:T(8,128)} fusion(f32[128,128]{0,1:T(8,128)S(1)} %copy.265, s32[16384]{0:T(1024)S(1)} %bitcast_clamp_fusion.2), kind=kCustom, calls=%fused_computation.clone.1 | custom fusion | bytes 16842752 | tf_op jit(solution)/shard_map/while/body/eval_jaxpr/jit(_take)/gather | solution.py:42
  1039.9 54.8 %gather_fusion = f32[16384,128]{1,0:T(8,128)} fusion(f32[128,128]{0,1:T(8,128)S(1)} %copy.265, s32[16384]{0:T(1024)S(1)} %bitcast_clamp_fusion.2), kind=kCustom, calls=%fused_computation.clone.1 | custom fusion | bytes 16842752 | tf_op jit(solution)/shard_map/while/body/eval_jaxpr/jit(_take)/gather | solution.py:42
  1127.8 54.8 %gather_fusion = f32[16384,128]{1,0:T(8,128)} fusion(f32[128,128]{0,1:T(8,128)S(1)} %copy.265, s32[16384]{0:T(1024)S(1)} %bitcast_clamp_fusion.2), kind=kCustom, calls=%fused_computation.clone.1 | custom fusion | bytes 16842752 | tf_op jit(solution)/shard_map/while/body/eval_jaxpr/jit(_take)/gather | solution.py:42
  1215.6 54.8 %gather_fusion = f32[16384,128]{1,0:T(8,128)} fusion(f32[128,128]{0,1:T(8,128)S(1)} %copy.265, s32[16384]{0:T(1024)S(1)} %bitcast_clamp_fusion.2), kind=kCustom, calls=%fused_computation.clone.1 | custom fusion | bytes 16842752 | tf_op jit(solution)/shard_map/while/body/eval_jaxpr/jit(_take)/gather | solution.py:42
  1303.5 54.8 %gather_fusion = f32[16384,128]{1,0:T(8,128)} fusion(f32[128,128]{0,1:T(8,128)S(1)} %copy.265, s32[16384]{0:T(1024)S(1)} %bitcast_clamp_fusion.2), kind=kCustom, calls=%fused_computation.clone.1 | custom fusion | bytes 16842752 | tf_op jit(solution)/shard_map/while/body/eval_jaxpr/jit(_take)/gather | solution.py:42
  1391.4 54.8 %gather_fusion = f32[16384,128]{1,0:T(8,128)} fusion(f32[128,128]{0,1:T(8,128)S(1)} %copy.265, s32[16384]{0:T(1024)S(1)} %bitcast_clamp_fusion.2), kind=kCustom, calls=%fused_computation.clone.1 | custom fusion | bytes 16842752 | tf_op jit(solution)/shard_map/while/body/eval_jaxpr/jit(_take)/gather | solution.py:42
  1479.2 54.8 %gather_fusion = f32[16384,128]{1,0:T(8,128)} fusion(f32[128,128]{0,1:T(8,128)S(1)} %copy.265, s32[16384]{0:T(1024)S(1)} %bitcast_clamp_fusion.2), kind=kCustom, calls=%fused_computation.clone.1 | custom fusion | bytes 16842752 | tf_op jit(solution)/shard_map/while/body/eval_jaxpr/jit(_take)/gather | solution.py:42
  1567.1 54.8 %gather_fusion = f32[16384,128]{1,0:T(8,128)} fusion(f32[128,128]{0,1:T(8,128)S(1)} %copy.265, s32[16384]{0:T(1024)S(1)} %bitcast_clamp_fusion.2), kind=kCustom, calls=%fused_computation.clone.1 | custom fusion | bytes 16842752 | tf_op jit(solution)/shard_map/while/body/eval_jaxpr/jit(_take)/gather | solution.py:42
  (304 shorter events, 602.7 us)
Async XLA Ops:
  7.2 35.8 %copy-start = (bf16[512,1024]{1,0:T(8,128)(2,1)S(1)}, bf16[512,1024]{1,0:T(8,128)(2,1)}, u32[]{:S(2)}) copy-start(bf16[512,1024]{1,0:T(8,128)(2,1)} %param.20) | copy-start | bytes 3145732
  7.2 4.4 copy-start.9
  7.2 99.6 %all-reduce.3.cloned.1.call-start = ((), (), s32[]{:S(2)}) async-start(), calls=%async_computation.6 | async-start | bytes 4194304
  11.5 2.5 copy-start.1
  11.5 2.6 copy-start.2
  11.6 0.6 copy-start.6
  42.2 0.7 copy-start.8
  42.2 16.5 copy-start.5
  42.2 100.9 %reduce-scatter.3.cloned.1.call-start = ((), (), s32[]{:S(2)}) async-start(), calls=%async_computation.2 | async-start | bytes 221184 | tf_op jit(solution)/shard_map/reduce_scatter | solution.py:136
  58.7 7.4 copy-start.10
  58.7 10.0 copy-start.3
  66.0 111.0 %reduce-scatter.5.cloned.1.call-start = ((), (), s32[]{:S(2)}) async-start(), calls=%async_computation.3 | async-start | bytes 40960 | tf_op jit(solution)/shard_map/reduce_scatter | solution.py:158
  157.9 2.8 copy-start.4
  157.9 42.5 %all-gather.7.cloned.1.call-start = ((), (), s32[]{:S(2)}) async-start(), calls=%async_computation.5 | async-start | bytes 1179648 | tf_op jit(solution)/shard_map/all_gather | solution.py:16
  158.5 71.6 %all-gather.5.cloned.1.call-start = ((), (), s32[]{:S(2)}) async-start(), calls=%async_computation.4 | async-start | bytes 2359296 | tf_op jit(solution)/shard_map/all_gather | solution.py:16
  163.3 10.5 copy-start.7
Sparse Core Ops, SparseCore 0:
  42.4 64.4 all-reduce.2
  110.4 32.6 reduce-scatter.2
  158.0 18.9 reduce-scatter.4
  178.7 21.6 all-gather.6
  202.2 27.8 all-gather.4
where the time goes:
time: 1670 us; the launch traced here: 1660 us
  local copies, waits for them, and re-layouts  1090 us (65%)
  matrix products  367 us (22%)
  waiting for transfers between devices  126 us (8%)
  other arithmetic  44.2 us (3%)
  blocking collectives  24.2 us (1%)
    gather x32, local copies, waits for them, and re-layouts, one_group(): jnp.take(filt, jnp.maximum(distance, 0), axis=1)  1030 us
    dot_general x16, matrix products, one_group(): inner = jnp.einsum('gij,bgnj->bgni', toeplitz, blocked, precision=highest)  247 us
    all_gather x2, waiting for transfers between devices, carried_in(): pieces = jax.tree.map(lambda part: lax.all_gather(part, axis), value)  51.8 us
    dot_general x16, matrix products, one_group(): jnp.einsum('mgj,bgnj->bmgn', tail_weight, blocked, precision=highest)  43.8 us
    unnamed x6, waiting for transfers between devices  37.4 us
    dot_general x16, matrix products, one_group(): jnp.einsum('mgi,bmgn->bgni', head_weight, carried, precision=highest)  36.8 us
    reduce_scatter x1, waiting for transfers between devices, body(): lax.psum_scatter(proj_terms, 'seq', scatter_dimension=2, tiled=True)  34.6 us
  transfers between devices with their start and end apart: 5, of which 5 were waited for; matrix products, arithmetic and copies ran while one was open for 2% of the time, Pallas kernels for 0%

commit v1 on v0

v1 whole, which is shorter than its diff:
```python
import functools

import jax
import jax.numpy as jnp
from jax import lax
from jax.experimental import pallas as pl
from jax.experimental.pallas import tpu as pltpu
from jax.sharding import PartitionSpec as P

LANES = 128
F32 = jnp.float32
BF16 = jnp.bfloat16
VMEM = pl.BlockSpec(memory_space=pltpu.VMEM)
ANY = pl.BlockSpec(memory_space=pl.ANY)
SMEM = pl.BlockSpec(memory_space=pltpu.SMEM)
LIMIT = 50 * 2**20


def first_kernel(
    seq_count, steps,
    feat, offsets, tokens, par, embedding, gain, weight,
    ut, send,
    kv, held, kv_sem, w_sem,
):
    _, batch, chans, length = feat.shape
    groups = chans // LANES
    modes = (par.shape[0] - 1) // 2
    per = max(1, groups // seq_count)
    kv_copy = pltpu.make_async_copy(feat.at[pl.ds(1, 2)], kv, kv_sem)
    kv_copy.start()
    w_copies = [
        pltpu.make_async_copy(weight.at[i], held.at[i], w_sem.at[i]) for i in range(3)
    ]
    for copy in w_copies:
        copy.start()

    count = tokens.shape[0]
    vocab = embedding.shape[0]
    hot = (tokens[...] == lax.broadcasted_iota(jnp.int32, (count, vocab), 1)).astype(F32).astype(BF16)
    rows = jnp.dot(hot, embedding[...], preferred_element_type=F32)
    squares = jnp.broadcast_to(jnp.sum(rows * rows, axis=1, keepdims=True), (count, LANES))
    scaled = rows * gain[...]
    high = scaled.astype(BF16)
    low = (scaled - high.astype(F32)).astype(BF16)
    both = jnp.concatenate([high.astype(F32), low.astype(F32)], axis=0).astype(BF16)
    base = batch * modes
    for j in range(groups // per):
        send[j, pl.ds((base + 3 * count) * per, count), :] = squares

    kv_copy.wait()
    start = lax.axis_index("seq") * length
    place = start + lax.broadcasted_iota(jnp.int32, (LANES, length), 1)

    def turn(g, carry):
        at = pl.ds(pl.multiple_of(g * LANES, LANES), LANES)
        for b in range(batch):
            product = kv[0, b, at, :].astype(F32) * kv[1, b, at, :].astype(F32)
            signal = jnp.where(place >= offsets[b], product, 0.0).astype(BF16).astype(F32)
            ut[b, pl.ds(g, length, stride=groups), :] = signal.T
        return carry

    lax.fori_loop(0, groups, turn, 0)

    for h in range(groups // 8):
        decay = [jnp.exp(-par[m, 8 * h : 8 * h + 8, :]) for m in range(modes)]

        def step(t, state):
            at = pl.ds(pl.multiple_of(t * groups + 8 * h, 8), 8)
            now = [ut[b, at, :] for b in range(batch)]
            return tuple(
                decay[m] * state[b * modes + m] + now[b]
                for b in range(batch)
                for m in range(modes)
            )

        zero = jnp.zeros((8, LANES), F32)
        ends = lax.fori_loop(0, length, step, (zero,) * base, unroll=4)
        for r in range(base):
            for g in range(8):
                j, at = divmod(8 * h + g, per)
                send[j, r * per + at, :] = ends[r][g]

    for i in range(3):
        w_copies[i].wait()
        for c in range(0, chans, 512):
            term = jnp.dot(both, held[i, :, c : c + 512], preferred_element_type=F32)
            term = term[:count] + term[count:]
            for g in range(4):
                j, at = divmod(c // LANES + g, per)
                first = (base + i * count) * per + at
                send[j, pl.ds(first, count, stride=per), :] = term[:, g * LANES : (g + 1) * LANES]


def exchange(mine, chan, seq_count, share, source, target, send_sem, recv_sem):
    target[mine] = source[lax.div(mine, share)]
    copies = []
    for d in range(1, seq_count):
        other = lax.rem(mine + d, seq_count)
        copies.append(
            pltpu.make_async_remote_copy(
                src_ref=source.at[lax.div(other, share)],
                dst_ref=target.at[mine],
                send_sem=send_sem.at[d - 1],
                recv_sem=recv_sem.at[d - 1],
                device_id=(other, chan),
                device_id_type=pl.DeviceIdType.MESH,
            )
        )
    for copy in copies:
        copy.start()
    return copies


def middle_kernel(
    seq_count, chan_count, batch, steps, modes, length, width,
    send, own, out_weight,
    carried, decoded,
    got, back, got_back, rows, spread, proj, scale, mix, part, got_part, held, w_sem,
    send_a, recv_a, send_b, recv_b, send_c, recv_c,
):
    mine, chan = lax.axis_index("seq"), lax.axis_index("chan")
    per = own.shape[0] // (2 * modes + 1)
    slots = send.shape[0]
    share = seq_count // slots
    count = batch * steps
    base = batch * modes
    block = modes * per
    w_copy = pltpu.make_async_copy(out_weight, held, w_sem)
    w_copy.start()
    barrier = pltpu.get_barrier_semaphore()
    for d in range(1, seq_count):
        pl.semaphore_signal(
            barrier, inc=1, device_id=(lax.rem(mine + d, seq_count), chan),
            device_id_type=pl.DeviceIdType.MESH,
        )
    for d in range(1, chan_count):
        pl.semaphore_signal(
            barrier, inc=1, device_id=(mine, lax.rem(chan + d, chan_count)),
            device_id_type=pl.DeviceIdType.MESH,
        )
    pl.semaphore_wait(barrier, seq_count + chan_count - 2)

    copies = exchange(mine, chan, seq_count, share, send, got, send_a, recv_a)
    rate = own[:block, :]
    decay = jnp.exp(-rate)
    power = jnp.exp(-rate * float(length))
    residue = own[block : 2 * block, :]
    skip = own[2 * block :, :]
    for copy in copies:
        copy.wait()

    state = []
    for b in range(batch):
        running = jnp.zeros((block, LANES), F32)
        for j in range(seq_count):
            back[j, b * block : (b + 1) * block, :] = running
            running = power * running + got[j, b * block : (b + 1) * block, :]
        state.append(running)

    first = base * per
    total = got[0, first : first + 3 * count * per, :]
    squares = got[0, first + 3 * count * per :, :]
    for j in range(1, seq_count):
        total = total + got[j, first : first + 3 * count * per, :]
        squares = squares + got[j, first + 3 * count * per :, :]
    proj[...] = total
    scale[...] = lax.rsqrt(squares / float(width) + 1e-05)

    def projected(i, token):
        at = (i * count + token) * per
        value = proj[at : at + per, :] * scale[token : token + 1, :]
        return value.astype(BF16).astype(F32)

    for b in range(batch):
        running = state[b]
        for s in range(steps):
            token = b * steps + s
            fed = (projected(1, token) * projected(2, token)).astype(BF16).astype(F32)
            for m in range(modes):
                spread[m * per : (m + 1) * per, :] = fed
            running = decay * running + spread[...]
            rows[...] = residue * running
            value = skip * fed
            for m in range(modes):
                value = value + rows[m * per : (m + 1) * per, :]
            value = (projected(0, token) * value).astype(BF16).astype(F32)
            at = first + token * per
            for j in range(seq_count):
                back[j, at : at + per, :] = value

    copies_back = exchange(mine, chan, seq_count, 1, back, got_back, send_b, recv_b)
    for copy in copies_back:
        copy.wait()
    for j in range(slots):
        for g in range(per):
            at = j * per + g
            mix[:, at * LANES : (at + 1) * LANES] = got_back[j * share, pl.ds(first + g, count, stride=per), :]
    w_copy.wait()
    piece = held.shape[1] // chan_count
    mixed = mix[...].astype(BF16)
    for c in range(chan_count):
        part[c] = jnp.dot(
            mixed, held[:, c * piece : (c + 1) * piece], preferred_element_type=F32
        )
    got_part[chan] = part[chan]
    sums = []
    for d in range(1, chan_count):
        other = lax.rem(chan + d, chan_count)
        sums.append(
            pltpu.make_async_remote_copy(
                src_ref=part.at[other],
                dst_ref=got_part.at[chan],
                send_sem=send_c.at[d - 1],
                recv_sem=recv_c.at[d - 1],
                device_id=(mine, other),
                device_id_type=pl.DeviceIdType.MESH,
            )
        )
    for copy in sums:
        copy.start()
    for j in range(slots):
        for r in range(base):
            carried[r, j * per : (j + 1) * per, :] = got_back[j * share, r * per : (r + 1) * per, :]
    for copy in sums:
        copy.wait()
    value = got_part[0]
    for c in range(1, chan_count):
        value = value + got_part[c]
    decoded[...] = value.astype(BF16)


def last_kernel(feat, ut, par, carried, mixed, query, conv, q_sem):
    _, batch, chans, length = feat.shape
    groups = chans // LANES
    modes = (par.shape[0] - 1) // 2
    q_copy = pltpu.make_async_copy(feat.at[0], query, q_sem)
    q_copy.start()
    for h in range(groups // 8):
        tile = slice(8 * h, 8 * h + 8)
        decay = [jnp.exp(-par[m, tile, :]) for m in range(modes)]
        residue = [par[modes + m, tile, :] for m in range(modes)]
        skip = par[2 * modes, tile, :]
        for b in range(batch):

            def step(t, state):
                at = pl.ds(pl.multiple_of(t * groups + 8 * h, 8), 8)
                now = ut[b, at, :]
                state = [decay[m] * state[m] + residue[m] * now for m in range(modes)]
                terms = list(state) + [skip * now]
                while len(terms) > 1:
                    pairs = [x + y for x, y in zip(terms[::2], terms[1::2])]
                    terms = pairs + terms[len(pairs) * 2 :]
                conv[b, at, :] = terms[0]
                return tuple(state)

            begin = tuple(residue[m] * carried[b * modes + m, tile, :] for m in range(modes))
            lax.fori_loop(0, length, step, begin, unroll=4)
    q_copy.wait()

    def turn(g, carry):
        at = pl.ds(pl.multiple_of(g * LANES, LANES), LANES)
        for b in range(batch):
            value = conv[b, pl.ds(g, length, stride=groups), :].T
            mixed[b, at, :] = (query[b, at, :].astype(F32) * value).astype(BF16)
        return carry

    lax.fori_loop(0, groups, turn, 0)


def body(
    features, offsets, tokens, decay_rate, residue, skip_weight,
    embedding, norm_gain, dec_weight, out_weight,
):
    seq_count, chan_count = lax.axis_size("seq"), lax.axis_size("chan")
    _, batch, chans, length = features.shape
    modes = decay_rate.shape[0]
    steps = tokens.shape[1]
    count = batch * steps
    groups = chans // LANES
    per = max(1, groups // seq_count)
    slots = groups // per
    depth = embedding.shape[1]
    base = batch * modes
    rows = (base + 3 * count) * per + count
    par = jnp.concatenate([decay_rate, residue, skip_weight[None]], axis=0)
    slot = lax.axis_index("seq") // (seq_count // slots)
    own = lax.dynamic_slice_in_dim(par, slot * per * LANES, per * LANES, 1)
    own = own.reshape((2 * modes + 1) * per, LANES)
    par = par.reshape(2 * modes + 1, groups, LANES)
    params = functools.partial(pltpu.CompilerParams, vmem_limit_bytes=LIMIT)

    ut, send = pl.pallas_call(
        functools.partial(first_kernel, seq_count, steps),
        out_shape=(
            jax.ShapeDtypeStruct((batch, length * groups, LANES), F32),
            jax.ShapeDtypeStruct((slots, rows, LANES), F32),
        ),
        in_specs=[ANY, SMEM, VMEM, VMEM, VMEM, VMEM, ANY],
        out_specs=(VMEM, VMEM),
        scratch_shapes=[
            pltpu.VMEM((2, batch, chans, length), BF16),
            pltpu.VMEM((3, depth, chans), BF16),
            pltpu.SemaphoreType.DMA,
            pltpu.SemaphoreType.DMA((3,)),
        ],
        compiler_params=params(),
        name="ends_and_projections",
    )(features, offsets, tokens.reshape(count, 1), par, embedding, norm_gain[None], dec_weight)

    out_width = out_weight.shape[1]
    back_rows = (base + count) * per
    carried, decoded = pl.pallas_call(
        functools.partial(
            middle_kernel, seq_count, chan_count, batch, steps, modes, length, depth * seq_count
        ),
        out_shape=(
            jax.ShapeDtypeStruct((base, groups, LANES), F32),
            jax.ShapeDtypeStruct((count, out_width // chan_count), BF16),
        ),
        in_specs=[VMEM, VMEM, ANY],
        out_specs=(VMEM, VMEM),
        scratch_shapes=[
            pltpu.VMEM((seq_count, rows, LANES), F32),
            pltpu.VMEM((seq_count, back_rows, LANES), F32),
            pltpu.VMEM((seq_count, back_rows, LANES), F32),
            pltpu.VMEM((modes * per, LANES), F32),
            pltpu.VMEM((modes * per, LANES), F32),
            pltpu.VMEM((3 * count * per, LANES), F32),
            pltpu.VMEM((count, LANES), F32),
            pltpu.VMEM((count, chans), F32),
            pltpu.VMEM((chan_count, count, out_width // chan_count), F32),
            pltpu.VMEM((chan_count, count, out_width // chan_count), F32),
            pltpu.VMEM(out_weight.shape, BF16),
            pltpu.SemaphoreType.DMA,
            pltpu.SemaphoreType.DMA((seq_count - 1,)),
            pltpu.SemaphoreType.DMA((seq_count - 1,)),
            pltpu.SemaphoreType.DMA((seq_count - 1,)),
            pltpu.SemaphoreType.DMA((seq_count - 1,)),
            pltpu.SemaphoreType.DMA((chan_count - 1,)),
            pltpu.SemaphoreType.DMA((chan_count - 1,)),
        ],
        compiler_params=params(collective_id=0, has_side_effects=True),
        name="exchange_and_decode",
    )(send, own, out_weight)

    mixed = pl.pallas_call(
        last_kernel,
        out_shape=jax.ShapeDtypeStruct((batch, chans, length), BF16),
        in_specs=[ANY, VMEM, VMEM, VMEM],
        out_specs=VMEM,
        scratch_shapes=[
            pltpu.VMEM((batch, chans, length), BF16),
            pltpu.VMEM((batch, length * groups, LANES), F32),
            pltpu.SemaphoreType.DMA,
        ],
        compiler_params=params(),
        name="conv_and_gate",
    )(features, ut, par, carried)
    return mixed, decoded.reshape(batch, steps, -1)


def solution(mesh):
    placed = (
        P(None, None, "chan", "seq"),
        P(),
        P(),
        P(None, "chan"),
        P(None, "chan"),
        P("chan"),
        P(None, "seq"),
        P("seq"),
        P(None, "seq", "chan"),
        P("chan", "seq"),
    )
    return jax.shard_map(
        body,
        mesh=mesh,
        in_specs=placed,
        out_specs=(P(None, "chan", "seq"), P(None, None, ("seq", "chan"))),
        check_vma=False,
    )
```

time: 1670 us -> 49.3 us (0.03)
  local copies, waits for them, and re-layouts: 1090 us -> 5.79 us
  matrix products: 367 us -> 0 us
  waiting for transfers between devices: 126 us -> 0 us
  other arithmetic: 44.2 us -> 1.46 us
  Pallas kernels: 0 us -> 41.1 us
  blocking collectives: 24.2 us -> 0 us
    gather x32 -> x0, local copies, waits for them, and re-layouts: 1030 us -> none  [one_group(): jnp.take(filt, jnp.maximum(distance, 0), axis=1)]
    dot_general x52 -> x0, matrix products: 367 us -> none  [the longest x16 247 us: one_group(): inner = jnp.einsum('gij,bgnj->bgni', toeplitz, blocked, precision=highest)]
    all_gather x2 -> x0, waiting for transfers between devices: 51.8 us -> none  [carried_in(): pieces = jax.tree.map(lambda part: lax.all_gather(part, axis), value)]
    pallas_call x0 -> x3, Pallas kernels: none -> 41.1 us  [the longest x1 22.1 us: body(): pl.pallas_call(functools.partial(middle_kernel, seq_count, chan_count, ba...]
    mul x40 -> x0, local copies, waits for them, and re-layouts: 39.9 us -> none  [the longest x16 13.6 us: one_group(): res_group[:, :, None] * jnp.exp(expo[:, :, None] * lag_pos)]
    unnamed x6 -> x0, waiting for transfers between devices: 37.4 us -> none
    reduce_scatter x2 -> x0, waiting for transfers between devices: 36.9 us -> none  [the longest x1 34.6 us: body(): lax.psum_scatter(proj_terms, 'seq', scatter_dimension=2, tiled=True)]
  transfers between devices with their start and end apart: 5 -> 0, of which waited for: 5 -> 0; matrix products, arithmetic and copies ran while one was open for 2% -> 0% of each run, Pallas kernels for 0% -> 0%
where the time goes in v1:
time: 49.3 us; the launch traced here: 49 us
  Pallas kernels  41.1 us (83%)
  local copies, waits for them, and re-layouts  5.79 us (12%)
  other arithmetic  1.46 us (3%)
  between operations  0.68 us (1%)
    pallas_call x1, Pallas kernels, body(): pl.pallas_call(functools.partial(middle_kernel, seq_count, chan_count, ba...  22.1 us
    pallas_call x1, Pallas kernels, body(): pl.pallas_call(functools.partial(first_kernel, seq_count, steps), out_sha...  10.5 us
    pallas_call x1, Pallas kernels, body(): pl.pallas_call(last_kernel, out_shape=jax.ShapeDtypeStruct((batch, chans,...  8.43 us
    unnamed x8, local copies, waits for them, and re-layouts  4.43 us
    concatenate x2, other arithmetic, body(): par = jnp.concatenate([decay_rate, residue, skip_weight[None]], axis=0)  1.46 us

profile of v1, /device:TPU:0, one launch (start us, length us, event | category | flops | bytes accessed | tf_op | source)
XLA Modules:
  0.0 49.0 jit_solution(17969455903688560305)
XLA Ops:
  0.6 0.8 %reshape.21.tokens = s32[8,1]{1,0:T(8,128)S(1)} reshape(s32[2,4]{1,0:T(2,128)} %param.12) | data formatting | bytes 64 | tf_op jit(solution)/shard_map/reshape | solution.py:308
  1.4 0.7 %fusion.1 = f32[33,256]{1,0:T(8,128)S(1)} fusion(s32[]{:T(128)S(6)} %select_n.6, f32[16,2048]{1,0:T(8,128)} %param.13, f32[16,2048]{1,0:T(8,128)} %param.14, f32[1,2048]{1,0:T(1,128)} %bitcast.12), kind=kLoop, calls=%fused_computation.5 | loop fusion | flops 16896 | bytes 304132 | tf_op jit(solution)/shard_map/concatenate | solution.py:285
  2.1 0.9 %copy.14 = f32[2,8,16,128]{3,2,1,0:T(8,128)S(1)} copy(f32[2,8,16,128]{3,1,2,0:T(8,128)} %bitcast.8) | data formatting | bytes 262144
  3.1 0.9 %copy.13 = f32[2,8,16,128]{3,2,1,0:T(8,128)S(1)} copy(f32[2,8,16,128]{3,1,2,0:T(8,128)} %bitcast.9) | data formatting | bytes 262144
  4.0 0.7 %pad_maximum_fusion.par = f32[33,16,128]{2,1,0:T(8,128)S(1)} fusion(f32[1,16,128]{2,1,0:T(8,128)} %bitcast.13, f32[16,16,128]{2,1,0:T(8,128)S(1)} %bitcast.10, f32[16,16,128]{2,1,0:T(8,128)S(1)} %bitcast.11), kind=kLoop, calls=%fused_computation.3 | loop fusion | flops 135168 | bytes 540672 | tf_op jit(solution)/shard_map/concatenate | solution.py:285
  4.7 0.0 copy-start
  4.7 1.2 %copy-done = bf16[512,1024]{1,0:T(8,128)(2,1)S(1)} copy-done((bf16[512,1024]{1,0:T(8,128)(2,1)S(1)}, bf16[512,1024]{1,0:T(8,128)(2,1)}, u32[]{:S(2)}) %copy-start) | copy-done | bytes 1048600
  6.0 0.0 copy-start.1
  6.0 0.7 %copy-done.1 = f32[1024]{0:T(1024)S(1)} copy-done((f32[1024]{0:T(1024)S(1)}, f32[1024]{0:T(1024)}, u32[]{:S(2)}) %copy-start.1) | copy-done | bytes 4120
  6.6 0.0 copy-start.2
  6.6 0.7 %copy-done.2 = s32[2]{0:T(128)S(1)} copy-done((s32[2]{0:T(128)S(1)}, s32[2]{0:T(128)}, u32[]{:S(2)}) %copy-start.2) | copy-done | bytes 32
  7.3 10.5 %ends_and_projections.1 = (f32[2,2048,128]{2,1,0:T(8,128)S(1)}, f32[8,120,128]{2,1,0:T(8,128)S(1)}) custom-call(bf16[3,2,2048,128]{3,2,1,0:T(8,128)(2,1)} %feat.3, s32[2]{0:T(128)S(1)} %copy-done.2, s32[8,1]{1,0:T(8,128)S(1)} %reshape.21.tokens, f32[33,16,128]{2,1,0:T(8,128)S(1)} %pad_maximum_fusion.par, bf16[512,1024]{1,0:T(8,128)(2,1)S(1)} %copy-done, ...), custom_call_target="tpu_custom_call" | custom-call | tf_op jit(solution)/shard_map/ends_and_projections/pallas_call | solution.py:292
  17.8 22.1 %exchange_and_decode.1 = (f32[32,16,128]{2,1,0:T(8,128)S(1)}, bf16[8,256]{1,0:T(8,128)(2,1)S(1)}) custom-call(f32[8,120,128]{2,1,0:T(8,128)S(1)} %get-tuple-element.7.send, f32[66,128]{1,0:T(8,128)S(1)} %reshape.19.own, bf16[2048,1024]{1,0:T(8,128)(2,1)} %out_weight.1), custom_call_target="tpu_custom_call" | custom-call | tf_op jit(solution)/shard_map/exchange_and_decode/pallas_call | solution.py:312
  39.9 8.4 %conv_and_gate.1 = bf16[2,2048,128]{2,1,0:T(8,128)(2,1)} custom-call(bf16[3,2,2048,128]{3,2,1,0:T(8,128)(2,1)} %feat.3, f32[2,2048,128]{2,1,0:T(8,128)S(1)} %get-tuple-element.6.ut, f32[33,16,128]{2,1,0:T(8,128)S(1)} %pad_maximum_fusion.par, f32[32,16,128]{2,1,0:T(8,128)S(1)} %get-tuple-element.8.carried), custom_call_target="tpu_custom_call" | custom-call | tf_op jit(solution)/shard_map/conv_and_gate/pallas_call | solution.py:346
  48.4 0.6 %reshape.20 = bf16[2,4,256]{2,1,0:T(4,128)(2,1)} reshape(bf16[8,256]{1,0:T(8,128)(2,1)S(1)} %get-tuple-element.9) | data formatting | bytes 8192 | tf_op jit(solution)/shard_map/reshape | solution.py:359
  (1 shorter events, 0.0 us)
Async XLA Ops:
  4.7 1.2 %copy-start = (bf16[512,1024]{1,0:T(8,128)(2,1)S(1)}, bf16[512,1024]{1,0:T(8,128)(2,1)}, u32[]{:S(2)}) copy-start(bf16[512,1024]{1,0:T(8,128)(2,1)} %embedding.1) | copy-start | bytes 3145732
  6.0 0.7 %copy-start.1 = (f32[1024]{0:T(1024)S(1)}, f32[1024]{0:T(1024)}, u32[]{:S(2)}) copy-start(f32[1024]{0:T(1024)} %param.17) | copy-start | bytes 12292
  6.6 0.7 %copy-start.2 = (s32[2]{0:T(128)S(1)}, s32[2]{0:T(128)}, u32[]{:S(2)}) copy-start(s32[2]{0:T(128)} %offsets.1) | copy-start | bytes 28

commit v2 on v0

v2 whole, which is shorter than its diff:
```python
import functools

import jax
import jax.numpy as jnp
from jax import lax
from jax.experimental import pallas as pl
from jax.experimental.pallas import tpu as pltpu
from jax.sharding import PartitionSpec as P

LANES = 128
F32 = jnp.float32
BF16 = jnp.bfloat16
VMEM = pl.BlockSpec(memory_space=pltpu.VMEM)
ANY = pl.BlockSpec(memory_space=pl.ANY)
SMEM = pl.BlockSpec(memory_space=pltpu.SMEM)
LIMIT = 56 * 2**20


def exchange(mine, chan, count, source, target, send_sem, recv_sem, axis="seq"):
    here = mine if axis == "seq" else chan
    copies = []
    for d in range(1, count):
        other = lax.rem(here + d, count)
        copies.append(
            pltpu.make_async_remote_copy(
                src_ref=source(other),
                dst_ref=target.at[here],
                send_sem=send_sem.at[d - 1],
                recv_sem=recv_sem.at[d - 1],
                device_id=(other, chan) if axis == "seq" else (mine, other),
                device_id_type=pl.DeviceIdType.MESH,
            )
        )
    for copy in copies:
        copy.start()
    return copies


def kernel(
    seq_count, chan_count,
    feat, offsets, tokens, rate_hbm, residue_hbm, skip_hbm, table_hbm, gain_hbm, weight, out_weight,
    mixed, decoded,
    held_feat, rate, residue, skip, table, gain, held, held_out,
    ut, par, own, squares, got_squares, ends_out, got_ends, proj_out, got_proj,
    pre, got_pre, carried, rows, spread, proj, dec, got_dec, mix, part, got_part,
    in_sem, w_sem, send_q, recv_q, send_e, recv_e, send_p, recv_p, send_b, recv_b,
    send_d, recv_d, send_c, recv_c,
):
    _, batch, chans, length = feat.shape
    groups = chans // LANES
    modes = rate.shape[0]
    steps = tokens.shape[1]
    count = batch * steps
    base = batch * modes
    per = max(1, groups // seq_count)
    slots = groups // per
    share = seq_count // slots
    block = modes * per
    width = gain.shape[1] * seq_count
    mine, chan = lax.axis_index("seq"), lax.axis_index("chan")

    ins = [
        pltpu.make_async_copy(source, target, in_sem.at[i])
        for i, (source, target) in enumerate(
            [(table_hbm, table), (gain_hbm, gain), (rate_hbm, rate), (residue_hbm, residue),
             (skip_hbm, skip), (feat.at[pl.ds(1, 2)], held_feat.at[pl.ds(1, 2)])]
        )
    ]
    w_copies = [pltpu.make_async_copy(weight.at[i], held.at[i], w_sem.at[i]) for i in range(3)]
    w_copies.append(pltpu.make_async_copy(feat.at[0], held_feat.at[0], w_sem.at[3]))
    w_copies.append(pltpu.make_async_copy(out_weight, held_out, w_sem.at[4]))
    for copy in ins + w_copies:
        copy.start()
    barrier = pltpu.get_barrier_semaphore()
    for d in range(1, seq_count):
        pl.semaphore_signal(
            barrier, inc=1, device_id=(lax.rem(mine + d, seq_count), chan),
            device_id_type=pl.DeviceIdType.MESH,
        )
    for d in range(1, chan_count):
        pl.semaphore_signal(
            barrier, inc=1, device_id=(mine, lax.rem(chan + d, chan_count)),
            device_id_type=pl.DeviceIdType.MESH,
        )

    vocab = table.shape[0]
    line = lax.broadcasted_iota(jnp.int32, (count, vocab), 0)
    wanted = jnp.zeros((count, vocab), jnp.int32)
    for t in range(count):
        wanted = jnp.where(line == t, tokens[t // steps, t % steps], wanted)
    hot = (wanted == lax.broadcasted_iota(jnp.int32, (count, vocab), 1)).astype(F32).astype(BF16)
    for copy in ins[:2]:
        copy.wait()
    embedded = jnp.dot(hot, table[...], preferred_element_type=F32)
    squares[...] = jnp.broadcast_to(
        jnp.sum(embedded * embedded, axis=1, keepdims=True), (count, LANES)
    )
    got_squares[mine] = squares[...]
    pl.semaphore_wait(barrier, seq_count + chan_count - 2)
    q_copies = exchange(
        mine, chan, seq_count, lambda i: squares, got_squares, send_q, recv_q
    )

    for copy in ins[2:]:
        copy.wait()
    for g in range(groups):
        lanes = slice(g * LANES, (g + 1) * LANES)
        par[pl.ds(g, modes, stride=groups), :] = rate[:, lanes]
        par[pl.ds(modes * groups + g, modes, stride=groups), :] = residue[:, lanes]
        par[2 * modes * groups + g : 2 * modes * groups + g + 1, :] = skip[:, lanes]

    place = mine * length + lax.broadcasted_iota(jnp.int32, (LANES, length), 1)

    def turn(g, carry):
        at = pl.ds(pl.multiple_of(g * LANES, LANES), LANES)
        for b in range(batch):
            product = held_feat[1, b, at, :].astype(F32) * held_feat[2, b, at, :].astype(F32)
            signal = jnp.where(place >= offsets[b], product, 0.0).astype(BF16).astype(F32)
            ut[b, pl.ds(g, length, stride=groups), :] = signal.T
        return carry

    lax.fori_loop(0, groups, turn, 0, unroll=2)

    def params(kind, h):
        first = kind * modes * groups + 8 * h
        return [par[first + m * groups : first + m * groups + 8, :] for m in range(modes)]

    for h in range(groups // 8):
        decay = [jnp.exp(-x) for x in params(0, h)]

        def end_step(t, state):
            at = pl.ds(pl.multiple_of(t * groups + 8 * h, 8), 8)
            now = [ut[b, at, :] for b in range(batch)]
            return tuple(
                decay[m] * state[b * modes + m] + now[b]
                for b in range(batch)
                for m in range(modes)
            )

        ends = lax.fori_loop(
            0, length, end_step, (jnp.zeros((8, LANES), F32),) * base, unroll=4
        )
        for r in range(base):
            for g in range(0, 8, per):
                ends_out[(8 * h + g) // per, r * per : (r + 1) * per, :] = ends[r][g : g + per]
    got_ends[mine] = ends_out[lax.div(mine, share)]
    e_copies = exchange(
        mine, chan, seq_count, lambda i: ends_out.at[lax.div(i, share)], got_ends, send_e, recv_e
    )

    for copy in q_copies:
        copy.wait()
    total = got_squares[0]
    for j in range(1, seq_count):
        total = total + got_squares[j]
    scale = lax.rsqrt(total / float(width) + 1e-05)[:, :1]
    normed = (embedded * scale * gain[...]).astype(BF16)

    def project(i):
        w_copies[i].wait()
        for c in range(0, chans, 512):
            term = jnp.dot(normed, held[i, :, c : c + 512], preferred_element_type=F32)
            for g in range(4):
                j, at = divmod(c // LANES + g, per)
                proj_out[j, pl.ds(i * count * per + at, count, stride=per), :] = term[
                    :, g * LANES : (g + 1) * LANES
                ]

    project(0)
    project(1)

    slot = lax.div(mine, share)
    for m in range(2 * modes + 1):
        own[m * per : (m + 1) * per, :] = par[pl.ds(m * groups + slot * per, per), :]
    own_rate = own[:block, :]
    power = jnp.exp(-own_rate * float(length))
    for copy in e_copies:
        copy.wait()
    final = []
    for b in range(batch):
        running = jnp.zeros((block, LANES), F32)
        for j in range(seq_count):
            pre[j, b * block : (b + 1) * block, :] = running
            running = power * running + got_ends[j, b * block : (b + 1) * block, :]
        final.append(running)
    got_pre[mine] = pre[mine]
    b_copies = exchange(mine, chan, seq_count, lambda i: pre.at[i], got_pre, send_b, recv_b)

    project(2)
    got_proj[mine] = proj_out[slot]
    p_copies = exchange(
        mine, chan, seq_count, lambda i: proj_out.at[lax.div(i, share)], got_proj, send_p, recv_p
    )

    for copy in b_copies:
        copy.wait()
    for j in range(slots):
        for r in range(base):
            carried[r, j * per : (j + 1) * per, :] = got_pre[j * share, r * per : (r + 1) * per, :]

    def convolve(h):
        decay = [jnp.exp(-x) for x in params(0, h)]
        weights = params(1, h)
        direct = par[2 * modes * groups + 8 * h : 2 * modes * groups + 8 * h + 8, :]
        for b in range(batch):

            def step(t, state):
                at = pl.ds(pl.multiple_of(t * groups + 8 * h, 8), 8)
                now = ut[b, at, :]
                state = [decay[m] * state[m] + weights[m] * now for m in range(modes)]
                terms = list(state) + [direct * now]
                while len(terms) > 1:
                    pairs = [x + y for x, y in zip(terms[::2], terms[1::2])]
                    terms = pairs + terms[len(pairs) * 2 :]
                ut[b, at, :] = terms[0]
                return tuple(state)

            begin = tuple(
                weights[m] * carried[b * modes + m, 8 * h : 8 * h + 8, :] for m in range(modes)
            )
            lax.fori_loop(0, length, step, begin, unroll=4)

    halves = groups // 8
    for h in range(halves // 2):
        convolve(h)

    for copy in p_copies:
        copy.wait()
    total = got_proj[0]
    for j in range(1, seq_count):
        total = total + got_proj[j]
    proj[...] = total.astype(BF16).astype(F32)
    own_decay = jnp.exp(-own_rate)
    own_residue = own[block : 2 * block, :]
    own_skip = own[2 * block : 2 * block + per, :]

    def projected(i, token):
        at = (i * count + token) * per
        return proj[at : at + per, :]

    for b in range(batch):
        running = final[b]
        for s in range(steps):
            token = b * steps + s
            fed = (projected(1, token) * projected(2, token)).astype(BF16).astype(F32)
            for m in range(modes):
                spread[m * per : (m + 1) * per, :] = fed
            running = own_decay * running + spread[...]
            rows[...] = own_residue * running
            value = own_skip * fed
            for m in range(modes):
                value = value + rows[m * per : (m + 1) * per, :]
            value = (projected(0, token) * value).astype(BF16).astype(F32)
            dec[token * per : (token + 1) * per, :] = value
    got_dec[mine] = dec[...]
    d_copies = exchange(mine, chan, seq_count, lambda i: dec, got_dec, send_d, recv_d)

    for h in range(halves // 2, halves):
        convolve(h)

    for copy in d_copies:
        copy.wait()
    for j in range(slots):
        for g in range(per):
            at = j * per + g
            mix[:, at * LANES : (at + 1) * LANES] = got_dec[j * share, pl.ds(g, count, stride=per), :]
    w_copies[4].wait()
    piece = held_out.shape[1] // chan_count
    decode_mix = mix[...].astype(BF16)
    for c in range(chan_count):
        part[c] = jnp.dot(
            decode_mix, held_out[:, c * piece : (c + 1) * piece], preferred_element_type=F32
        )
    got_part[chan] = part[chan]
    c_copies = exchange(
        mine, chan, chan_count, lambda i: part.at[i], got_part, send_c, recv_c, "chan"
    )

    w_copies[3].wait()

    def gate(g, carry):
        at = pl.ds(pl.multiple_of(g * LANES, LANES), LANES)
        for b in range(batch):
            value = ut[b, pl.ds(g, length, stride=groups), :].T
            mixed[b, at, :] = (held_feat[0, b, at, :].astype(F32) * value).astype(BF16)
        return carry

    lax.fori_loop(0, groups, gate, 0, unroll=2)

    for copy in c_copies:
        copy.wait()
    value = got_part[0]
    for c in range(1, chan_count):
        value = value + got_part[c]
    decoded[...] = value.astype(BF16)


def body(
    features, offsets, tokens, decay_rate, residue, skip_weight,
    embedding, norm_gain, dec_weight, out_weight,
):
    seq_count, chan_count = lax.axis_size("seq"), lax.axis_size("chan")
    _, batch, chans, length = features.shape
    modes = decay_rate.shape[0]
    steps = tokens.shape[1]
    count = batch * steps
    groups = chans // LANES
    per = max(1, groups // seq_count)
    slots = groups // per
    base = batch * modes
    out_width = out_weight.shape[1]
    piece = out_width // chan_count

    def wide(*shape):
        return pltpu.VMEM(shape, F32)

    def sems(number):
        return pltpu.SemaphoreType.DMA((number,))

    mixed, decoded = pl.pallas_call(
        functools.partial(kernel, seq_count, chan_count),
        out_shape=(
            jax.ShapeDtypeStruct((batch, chans, length), BF16),
            jax.ShapeDtypeStruct((count, piece), BF16),
        ),
        in_specs=[ANY, SMEM, SMEM, ANY, ANY, ANY, ANY, ANY, ANY, ANY],
        out_specs=(VMEM, VMEM),
        scratch_shapes=[
            pltpu.VMEM(features.shape, BF16),
            wide(modes, chans),
            wide(modes, chans),
            wide(1, chans),
            pltpu.VMEM(embedding.shape, BF16),
            wide(1, norm_gain.shape[0]),
            pltpu.VMEM(dec_weight.shape, BF16),
            pltpu.VMEM(out_weight.shape, BF16),
            wide(batch, length * groups, LANES),
            wide((2 * modes + 1) * groups, LANES),
            wide((2 * modes + 1) * per, LANES),
            wide(count, LANES),
            wide(seq_count, count, LANES),
            wide(slots, base * per, LANES),
            wide(seq_count, base * per, LANES),
            wide(slots, 3 * count * per, LANES),
            wide(seq_count, 3 * count * per, LANES),
            wide(seq_count, base * per, LANES),
            wide(seq_count, base * per, LANES),
            wide(base, groups, LANES),
            wide(modes * per, LANES),
            wide(modes * per, LANES),
            wide(3 * count * per, LANES),
            wide(count * per, LANES),
            wide(seq_count, count * per, LANES),
            wide(count, chans),
            wide(chan_count, count, piece),
            wide(chan_count, count, piece),
            sems(6),
            sems(5),
        ]
        + [sems(seq_count - 1)] * 10
        + [sems(chan_count - 1)] * 2,
        compiler_params=pltpu.CompilerParams(
            vmem_limit_bytes=LIMIT, collective_id=0, has_side_effects=True
        ),
        name="layer",
    )(
        features, offsets, tokens, decay_rate, residue, skip_weight[None],
        embedding, norm_gain[None], dec_weight, out_weight,
    )
    return mixed, decoded.reshape(batch, steps, -1)


def solution(mesh):
    placed = (
        P(None, None, "chan", "seq"),
        P(),
        P(),
        P(None, "chan"),
        P(None, "chan"),
        P("chan"),
        P(None, "seq"),
        P("seq"),
        P(None, "seq", "chan"),
        P("chan", "seq"),
    )
    return jax.shard_map(
        body,
        mesh=mesh,
        in_specs=placed,
        out_specs=(P(None, "chan", "seq"), P(None, None, ("seq", "chan"))),
        check_vma=False,
    )
```

time: 1670 us -> 39.1 us (0.02)
  local copies, waits for them, and re-layouts: 1090 us -> 3.54 us
  matrix products: 367 us -> 0 us
  waiting for transfers between devices: 126 us -> 0 us
  other arithmetic: 44.2 us -> 0 us
  Pallas kernels: 0 us -> 34.7 us
  blocking collectives: 24.2 us -> 0 us
    gather x32 -> x0, local copies, waits for them, and re-layouts: 1030 us -> none  [one_group(): jnp.take(filt, jnp.maximum(distance, 0), axis=1)]
    dot_general x52 -> x0, matrix products: 367 us -> none  [the longest x16 247 us: one_group(): inner = jnp.einsum('gij,bgnj->bgni', toeplitz, blocked, precision=highest)]
    all_gather x2 -> x0, waiting for transfers between devices: 51.8 us -> none  [carried_in(): pieces = jax.tree.map(lambda part: lax.all_gather(part, axis), value)]
    mul x40 -> x0, local copies, waits for them, and re-layouts: 39.9 us -> none  [the longest x16 13.6 us: one_group(): res_group[:, :, None] * jnp.exp(expo[:, :, None] * lag_pos)]
    unnamed x6 -> x0, waiting for transfers between devices: 37.4 us -> none
    reduce_scatter x2 -> x0, waiting for transfers between devices: 36.9 us -> none  [the longest x1 34.6 us: body(): lax.psum_scatter(proj_terms, 'seq', scatter_dimension=2, tiled=True)]
    pallas_call x0 -> x1, Pallas kernels: none -> 34.7 us  [body(): pl.pallas_call(functools.partial(kernel, seq_count, chan_count), out_shap...]
  transfers between devices with their start and end apart: 5 -> 0, of which waited for: 5 -> 0; matrix products, arithmetic and copies ran while one was open for 2% -> 0% of each run, Pallas kernels for 0% -> 0%
where the time goes in v2:
time: 39.1 us; the launch traced here: 38.8 us
  Pallas kernels  34.7 us (89%)
  local copies, waits for them, and re-layouts  3.54 us (9%)
  between operations  0.64 us (2%)
    pallas_call x1, Pallas kernels, body(): pl.pallas_call(functools.partial(kernel, seq_count, chan_count), out_shap...  34.7 us
    unnamed x1, local copies, waits for them, and re-layouts  2.26 us
    reshape x1, local copies, waits for them, and re-layouts, body(): return (mixed, decoded.reshape(batch, steps, -1))  1.28 us

profile of v2, /device:TPU:0, one launch (start us, length us, event | category | flops | bytes accessed | tf_op | source)
XLA Modules:
  0.0 38.8 jit_solution(10950725755595500739)
XLA Ops:
  0.6 34.7 %layer.1 = (bf16[2,2048,128]{2,1,0:T(8,128)(2,1)}, bf16[8,256]{1,0:T(8,128)(2,1)}) custom-call(bf16[3,2,2048,128]{3,2,1,0:T(8,128)(2,1)} %feat.1, s32[2]{0:T(128)} %offsets.1, s32[2,4]{1,0:T(2,128)} %tokens.1, f32[16,2048]{1,0:T(8,128)} %rate_hbm.1, f32[16,2048]{1,0:T(8,128)} %residue_hbm.1, f32[1,2048]{1,0:T(1,128)} %bitcast.2, ...), custom_call_target="tpu_custom_call" | custom-call | tf_op jit(solution)/shard_map/layer/pallas_call | solution.py:320
  35.3 1.3 %reshape.7 = bf16[2,4,256]{2,1,0:T(4,128)(2,1)} reshape(bf16[8,256]{1,0:T(8,128)(2,1)} %get-tuple-element.5) | data formatting | bytes 8192 | tf_op jit(solution)/shard_map/reshape | solution.py:370
  36.6 2.3 %copy.13 = bf16[2,2048,128]{2,1,0:T(8,128)(2,1)} copy(bf16[2,2048,128]{2,1,0:T(8,128)(2,1)} %get-tuple-element.8) | data formatting | bytes 2097152

commit v3 on v2

--- a/solution.py
+++ b/solution.py
@@ -39,11 +39,11 @@
 def kernel(
     seq_count, chan_count,
     feat, offsets, tokens, rate_hbm, residue_hbm, skip_hbm, table_hbm, gain_hbm, weight, out_weight,
-    mixed, decoded,
+    conv, decoded,
     held_feat, rate, residue, skip, table, gain, held, held_out,
     ut, par, own, squares, got_squares, ends_out, got_ends, proj_out, got_proj,
     pre, got_pre, carried, rows, spread, proj, dec, got_dec, mix, part, got_part,
-    in_sem, w_sem, send_q, recv_q, send_e, recv_e, send_p, recv_p, send_b, recv_b,
+    in_sem, w_sem, out_sem, send_q, recv_q, send_e, recv_e, send_p, recv_p, send_b, recv_b,
     send_d, recv_d, send_c, recv_c,
 ):
     _, batch, chans, length = feat.shape
@@ -63,12 +63,11 @@
         pltpu.make_async_copy(source, target, in_sem.at[i])
         for i, (source, target) in enumerate(
             [(table_hbm, table), (gain_hbm, gain), (rate_hbm, rate), (residue_hbm, residue),
-             (skip_hbm, skip), (feat.at[pl.ds(1, 2)], held_feat.at[pl.ds(1, 2)])]
+             (skip_hbm, skip), (feat.at[pl.ds(1, 2)], held_feat)]
         )
     ]
     w_copies = [pltpu.make_async_copy(weight.at[i], held.at[i], w_sem.at[i]) for i in range(3)]
-    w_copies.append(pltpu.make_async_copy(feat.at[0], held_feat.at[0], w_sem.at[3]))
-    w_copies.append(pltpu.make_async_copy(out_weight, held_out, w_sem.at[4]))
+    w_copies.append(pltpu.make_async_copy(out_weight, held_out, w_sem.at[3]))
     for copy in ins + w_copies:
         copy.start()
     barrier = pltpu.get_barrier_semaphore()
@@ -114,7 +113,7 @@
     def turn(g, carry):
         at = pl.ds(pl.multiple_of(g * LANES, LANES), LANES)
         for b in range(batch):
-            product = held_feat[1, b, at, :].astype(F32) * held_feat[2, b, at, :].astype(F32)
+            product = held_feat[0, b, at, :].astype(F32) * held_feat[1, b, at, :].astype(F32)
             signal = jnp.where(place >= offsets[b], product, 0.0).astype(BF16).astype(F32)
             ut[b, pl.ds(g, length, stride=groups), :] = signal.T
         return carry
@@ -125,8 +124,29 @@
         first = kind * modes * groups + 8 * h
         return [par[first + m * groups : first + m * groups + 8, :] for m in range(modes)]
 
-    for h in range(groups // 8):
+    def project(i, chunk):
+        columns = pl.ds(pl.multiple_of(chunk * 2 * LANES, 2 * LANES), 2 * LANES)
+        term = jnp.dot(normed, held[i, :, columns], preferred_element_type=F32)
+        for g in range(2):
+            j, at = chunk * (2 // per) + g // per, g % per
+            proj_out[j, pl.ds(i * count * per + at, count, stride=per), :] = term[
+                :, g * LANES : (g + 1) * LANES
+            ]
+
+    chunks = groups // 2
+    halves = groups // 8
+    for h in range(halves):
+        if h == halves - 1:
+            for copy in q_copies:
+                copy.wait()
+            total = got_squares[0]
+            for j in range(1, seq_count):
+                total = total + got_squares[j]
+            scale = lax.rsqrt(total / float(width) + 1e-05)[:, :1]
+            normed = (embedded * scale * gain[...]).astype(BF16)
+            w_copies[0].wait()
         decay = [jnp.exp(-x) for x in params(0, h)]
+        zero = jnp.zeros((8, LANES), F32)
 
         def end_step(t, state):
             at = pl.ds(pl.multiple_of(t * groups + 8 * h, 8), 8)
@@ -137,9 +157,16 @@
                 for m in range(modes)
             )
 
-        ends = lax.fori_loop(
-            0, length, end_step, (jnp.zeros((8, LANES), F32),) * base, unroll=4
-        )
+        def end_steps(chunk, state):
+            project(0, chunk)
+            for t in range(length // chunks):
+                state = end_step(chunk * (length // chunks) + t, state)
+            return state
+
+        if h == halves - 1:
+            ends = lax.fori_loop(0, chunks, end_steps, (zero,) * base)
+        else:
+            ends = lax.fori_loop(0, length, end_step, (zero,) * base, unroll=4)
         for r in range(base):
             for g in range(0, 8, per):
                 ends_out[(8 * h + g) // per, r * per : (r + 1) * per, :] = ends[r][g : g + per]
@@ -148,26 +175,9 @@
         mine, chan, seq_count, lambda i: ends_out.at[lax.div(i, share)], got_ends, send_e, recv_e
     )
 
-    for copy in q_copies:
-        copy.wait()
-    total = got_squares[0]
-    for j in range(1, seq_count):
-        total = total + got_squares[j]
-    scale = lax.rsqrt(total / float(width) + 1e-05)[:, :1]
-    normed = (embedded * scale * gain[...]).astype(BF16)
-
-    def project(i):
-        w_copies[i].wait()
-        for c in range(0, chans, 512):
-            term = jnp.dot(normed, held[i, :, c : c + 512], preferred_element_type=F32)
-            for g in range(4):
-                j, at = divmod(c // LANES + g, per)
-                proj_out[j, pl.ds(i * count * per + at, count, stride=per), :] = term[
-                    :, g * LANES : (g + 1) * LANES
-                ]
-
-    project(0)
-    project(1)
+    w_copies[1].wait()
+    for chunk in range(chunks):
+        project(1, chunk)
 
     slot = lax.div(mine, share)
     for m in range(2 * modes + 1):
@@ -186,7 +196,9 @@
     got_pre[mine] = pre[mine]
     b_copies = exchange(mine, chan, seq_count, lambda i: pre.at[i], got_pre, send_b, recv_b)
 
-    project(2)
+    w_copies[2].wait()
+    for chunk in range(chunks):
+        project(2, chunk)
     got_proj[mine] = proj_out[slot]
     p_copies = exchange(
         mine, chan, seq_count, lambda i: proj_out.at[lax.div(i, share)], got_proj, send_p, recv_p
@@ -198,31 +210,37 @@
         for r in range(base):
             carried[r, j * per : (j + 1) * per, :] = got_pre[j * share, r * per : (r + 1) * per, :]
 
-    def convolve(h):
+    def convolve(b, h):
         decay = [jnp.exp(-x) for x in params(0, h)]
         weights = params(1, h)
         direct = par[2 * modes * groups + 8 * h : 2 * modes * groups + 8 * h + 8, :]
-        for b in range(batch):
-
-            def step(t, state):
-                at = pl.ds(pl.multiple_of(t * groups + 8 * h, 8), 8)
-                now = ut[b, at, :]
-                state = [decay[m] * state[m] + weights[m] * now for m in range(modes)]
-                terms = list(state) + [direct * now]
-                while len(terms) > 1:
-                    pairs = [x + y for x, y in zip(terms[::2], terms[1::2])]
-                    terms = pairs + terms[len(pairs) * 2 :]
-                ut[b, at, :] = terms[0]
-                return tuple(state)
-
-            begin = tuple(
-                weights[m] * carried[b * modes + m, 8 * h : 8 * h + 8, :] for m in range(modes)
-            )
-            lax.fori_loop(0, length, step, begin, unroll=4)
-
-    halves = groups // 8
-    for h in range(halves // 2):
-        convolve(h)
+
+        def step(t, state):
+            at = pl.ds(pl.multiple_of(t * groups + 8 * h, 8), 8)
+            now = ut[b, at, :]
+            state = [decay[m] * state[m] + weights[m] * now for m in range(modes)]
+            terms = list(state) + [direct * now]
+            while len(terms) > 1:
+                pairs = [x + y for x, y in zip(terms[::2], terms[1::2])]
+                terms = pairs + terms[len(pairs) * 2 :]
+            ut[b, at, :] = terms[0]
+            return tuple(state)
+
+        begin = tuple(
+            weights[m] * carried[b * modes + m, 8 * h : 8 * h + 8, :] for m in range(modes)
+        )
+        lax.fori_loop(0, length, step, begin, unroll=4)
+
+    units = [(b, h) for b in range(batch) for h in range(halves)]
+    conv_copies = [pltpu.make_async_copy(ut.at[b], conv.at[b], out_sem.at[b]) for b in range(batch)]
+
+    def run(first, stop):
+        for b, h in units[first:stop]:
+            convolve(b, h)
+            if h == halves - 1:
+                conv_copies[b].start()
+
+    run(0, 1)
 
     for copy in p_copies:
         copy.wait()
@@ -255,8 +273,7 @@
     got_dec[mine] = dec[...]
     d_copies = exchange(mine, chan, seq_count, lambda i: dec, got_dec, send_d, recv_d)
 
-    for h in range(halves // 2, halves):
-        convolve(h)
+    run(1, len(units) - 1)
 
     for copy in d_copies:
         copy.wait()
@@ -264,7 +281,7 @@
         for g in range(per):
             at = j * per + g
             mix[:, at * LANES : (at + 1) * LANES] = got_dec[j * share, pl.ds(g, count, stride=per), :]
-    w_copies[4].wait()
+    w_copies[3].wait()
     piece = held_out.shape[1] // chan_count
     decode_mix = mix[...].astype(BF16)
     for c in range(chan_count):
@@ -276,23 +293,30 @@
         mine, chan, chan_count, lambda i: part.at[i], got_part, send_c, recv_c, "chan"
     )
 
-    w_copies[3].wait()
-
-    def gate(g, carry):
-        at = pl.ds(pl.multiple_of(g * LANES, LANES), LANES)
-        for b in range(batch):
-            value = ut[b, pl.ds(g, length, stride=groups), :].T
-            mixed[b, at, :] = (held_feat[0, b, at, :].astype(F32) * value).astype(BF16)
-        return carry
-
-    lax.fori_loop(0, groups, gate, 0, unroll=2)
-
+    run(len(units) - 1, len(units))
     for copy in c_copies:
         copy.wait()
     value = got_part[0]
     for c in range(1, chan_count):
         value = value + got_part[c]
-    decoded[...] = value.astype(BF16)
+    value = value.astype(BF16)
+    for b in range(batch):
+        decoded[b] = value[b * steps : (b + 1) * steps]
+    for copy in conv_copies:
+        copy.wait()
+
+
+def gate(query, conv, mixed):
+    _, _, chans, length = query.shape
+    groups = chans // LANES
+
+    def turn(g, carry):
+        at = pl.ds(pl.multiple_of(g * LANES, LANES), LANES)
+        value = conv[0, pl.ds(g, length, stride=groups), :].T
+        mixed[0, at, :] = (query[0, 0, at, :].astype(F32) * value).astype(BF16)
+        return carry
+
+    lax.fori_loop(0, groups, turn, 0, unroll=4)
 
 
 def body(
@@ -317,16 +341,16 @@
     def sems(number):
         return pltpu.SemaphoreType.DMA((number,))
 
-    mixed, decoded = pl.pallas_call(
+    conv, decoded = pl.pallas_call(
         functools.partial(kernel, seq_count, chan_count),
         out_shape=(
-            jax.ShapeDtypeStruct((batch, chans, length), BF16),
-            jax.ShapeDtypeStruct((count, piece), BF16),
+            jax.ShapeDtypeStruct((batch, length * groups, LANES), F32),
+            jax.ShapeDtypeStruct((batch, steps, piece), BF16),
         ),
         in_specs=[ANY, SMEM, SMEM, ANY, ANY, ANY, ANY, ANY, ANY, ANY],
-        out_specs=(VMEM, VMEM),
+        out_specs=(ANY, VMEM),
         scratch_shapes=[
-            pltpu.VMEM(features.shape, BF16),
+            pltpu.VMEM((2,) + features.shape[1:], BF16),
             wide(modes, chans),
             wide(modes, chans),
             wide(1, chans),
@@ -355,7 +379,8 @@
             wide(chan_count, count, piece),
             wide(chan_count, count, piece),
             sems(6),
-            sems(5),
+            sems(4),
+            sems(batch),
         ]
         + [sems(seq_count - 1)] * 10
         + [sems(chan_count - 1)] * 2,
@@ -367,7 +392,19 @@
         features, offsets, tokens, decay_rate, residue, skip_weight[None],
         embedding, norm_gain[None], dec_weight, out_weight,
     )
-    return mixed, decoded.reshape(batch, steps, -1)
+    mixed = pl.pallas_call(
+        gate,
+        grid=(batch,),
+        out_shape=jax.ShapeDtypeStruct((batch, chans, length), BF16),
+        in_specs=[
+            pl.BlockSpec((1, 1, chans, length), lambda b: (0, b, 0, 0)),
+            pl.BlockSpec((1, length * groups, LANES), lambda b: (b, 0, 0)),
+        ],
+        out_specs=pl.BlockSpec((1, chans, length), lambda b: (b, 0, 0)),
+        compiler_params=pltpu.CompilerParams(vmem_limit_bytes=LIMIT),
+        name="gate",
+    )(features, conv)
+    return mixed, decoded
 
 
 def solution(mesh):

time: 39.1 us -> 40.8 us (1.043)
  Pallas kernels: 34.7 us -> 39.4 us
  local copies, waits for them, and re-layouts: 3.54 us -> 0.6 us
    pallas_call x0 -> x1, Pallas kernels: none -> 3.35 us  [body(): pl.pallas_call(gate, grid=(batch,), out_shape=jax.ShapeDtypeStruct((batch...]
    unnamed x1 -> x3, local copies, waits for them, and re-layouts: 2.26 us -> 0.6 us
    pallas_call x1, Pallas kernels: 34.7 us -> 36 us  [body(): pl.pallas_call(functools.partial(kernel, seq_count, chan_count), out_shap...]
    reshape x1 -> x0, local copies, waits for them, and re-layouts: 1.28 us -> none  [body(): return (mixed, decoded.reshape(batch, steps, -1))]
where the time goes in v3:
time: 40.8 us; the launch traced here: 40.6 us
  Pallas kernels  39.4 us (97%)
  between operations  0.65 us (2%)
  local copies, waits for them, and re-layouts  0.6 us (1%)
    pallas_call x1, Pallas kernels, body(): pl.pallas_call(functools.partial(kernel, seq_count, chan_count), out_shap...  36 us
    pallas_call x1, Pallas kernels, body(): pl.pallas_call(gate, grid=(batch,), out_shape=jax.ShapeDtypeStruct((batch...  3.35 us

profile of v3, /device:TPU:0, one launch (start us, length us, event | category | flops | bytes accessed | tf_op | source)
XLA Modules:
  0.0 40.6 jit_solution(4265743393957525971)
XLA Ops:
  0.6 36.0 %layer.1 = (f32[2,2048,128]{2,1,0:T(8,128)}, bf16[2,4,256]{2,1,0:T(4,128)(2,1)}) custom-call(bf16[3,2,2048,128]{3,2,1,0:T(8,128)(2,1)} %query.1, s32[2]{0:T(128)} %offsets.1, s32[2,4]{1,0:T(2,128)} %tokens.1, f32[16,2048]{1,0:T(8,128)} %rate_hbm.1, f32[16,2048]{1,0:T(8,128)} %residue_hbm.1, f32[1,2048]{1,0:T(1,128)} %bitcast.2, bf16[512,1024]{1,0:T(8,128)(2,1)} %table_hbm.1, ...), custom_call_target="tpu_custom_call" | custom-call | tf_op jit(solution)/shard_map/layer/pallas_call | solution.py:344
  36.7 0.0 copy-start
  36.7 3.3 %gate.1 = bf16[2,2048,128]{2,1,0:T(8,128)(2,1)} custom-call(bf16[3,2,2048,128]{3,2,1,0:T(8,128)(2,1)} %query.1, f32[2,2048,128]{2,1,0:T(8,128)} %get-tuple-element.4.conv), custom_call_target="tpu_custom_call" | custom-call | tf_op jit(solution)/shard_map/gate/pallas_call | solution.py:395
  40.0 0.0 copy-done
  40.1 0.6 %copy.13 = bf16[2,4,256]{2,1,0:T(4,128)(2,1)} copy(bf16[2,4,256]{2,1,0:T(4,128)(2,1)S(1)} %copy-done) | data formatting | bytes 8192
Async XLA Ops:
  36.7 3.4 %copy-start = (bf16[2,4,256]{2,1,0:T(4,128)(2,1)S(1)}, bf16[2,4,256]{2,1,0:T(4,128)(2,1)}, u32[]{:S(2)}) copy-start(bf16[2,4,256]{2,1,0:T(4,128)(2,1)} %get-tuple-element.9) | copy-start | bytes 12292

commit v4 on v2

--- a/solution.py
+++ b/solution.py
@@ -16,17 +16,18 @@
 LIMIT = 56 * 2**20
 
 
-def exchange(mine, chan, count, source, target, send_sem, recv_sem, axis="seq"):
+def exchange(mine, chan, count, source, target, send_sem, recv_sem, axis="seq", part=None):
     here = mine if axis == "seq" else chan
+    first = 0 if part is None else part[0] * (count - 1)
     copies = []
     for d in range(1, count):
         other = lax.rem(here + d, count)
         copies.append(
             pltpu.make_async_remote_copy(
                 src_ref=source(other),
-                dst_ref=target.at[here],
-                send_sem=send_sem.at[d - 1],
-                recv_sem=recv_sem.at[d - 1],
+                dst_ref=target.at[here] if part is None else target.at[here, pl.ds(*part[1:])],
+                send_sem=send_sem.at[first + d - 1],
+                recv_sem=recv_sem.at[first + d - 1],
                 device_id=(other, chan) if axis == "seq" else (mine, other),
                 device_id_type=pl.DeviceIdType.MESH,
             )
@@ -125,28 +126,31 @@
         first = kind * modes * groups + 8 * h
         return [par[first + m * groups : first + m * groups + 8, :] for m in range(modes)]
 
-    for h in range(groups // 8):
-        decay = [jnp.exp(-x) for x in params(0, h)]
-
-        def end_step(t, state):
-            at = pl.ds(pl.multiple_of(t * groups + 8 * h, 8), 8)
-            now = [ut[b, at, :] for b in range(batch)]
-            return tuple(
-                decay[m] * state[b * modes + m] + now[b]
-                for b in range(batch)
-                for m in range(modes)
+    def part_of(b):
+        return (b, b * block, block)
+
+    e_copies = []
+    for b in range(batch):
+        for h in range(groups // 8):
+            decay = [jnp.exp(-x) for x in params(0, h)]
+
+            def end_step(t, state):
+                now = ut[b, pl.ds(pl.multiple_of(t * groups + 8 * h, 8), 8), :]
+                return tuple(decay[m] * state[m] + now for m in range(modes))
+
+            ends = lax.fori_loop(
+                0, length, end_step, (jnp.zeros((8, LANES), F32),) * modes, unroll=8
             )
-
-        ends = lax.fori_loop(
-            0, length, end_step, (jnp.zeros((8, LANES), F32),) * base, unroll=4
-        )
-        for r in range(base):
-            for g in range(0, 8, per):
-                ends_out[(8 * h + g) // per, r * per : (r + 1) * per, :] = ends[r][g : g + per]
-    got_ends[mine] = ends_out[lax.div(mine, share)]
-    e_copies = exchange(
-        mine, chan, seq_count, lambda i: ends_out.at[lax.div(i, share)], got_ends, send_e, recv_e
-    )
+            for m in range(modes):
+                r = b * modes + m
+                for g in range(0, 8, per):
+                    ends_out[(8 * h + g) // per, r * per : (r + 1) * per, :] = ends[m][g : g + per]
+        rows_of = pl.ds(b * block, block)
+        got_ends[mine, rows_of, :] = ends_out[lax.div(mine, share), rows_of, :]
+        e_copies.append(exchange(
+            mine, chan, seq_count, lambda i: ends_out.at[lax.div(i, share), rows_of], got_ends,
+            send_e, recv_e, part=part_of(b),
+        ))
 
     for copy in q_copies:
         copy.wait()
@@ -167,42 +171,47 @@
                 ]
 
     project(0)
-    project(1)
 
     slot = lax.div(mine, share)
     for m in range(2 * modes + 1):
         own[m * per : (m + 1) * per, :] = par[pl.ds(m * groups + slot * per, per), :]
     own_rate = own[:block, :]
     power = jnp.exp(-own_rate * float(length))
-    for copy in e_copies:
-        copy.wait()
-    final = []
+    final, b_copies = [], []
     for b in range(batch):
+        for copy in e_copies[b]:
+            copy.wait()
         running = jnp.zeros((block, LANES), F32)
+        rows_of = pl.ds(b * block, block)
         for j in range(seq_count):
             pre[j, b * block : (b + 1) * block, :] = running
             running = power * running + got_ends[j, b * block : (b + 1) * block, :]
         final.append(running)
-    got_pre[mine] = pre[mine]
-    b_copies = exchange(mine, chan, seq_count, lambda i: pre.at[i], got_pre, send_b, recv_b)
-
+        got_pre[mine, rows_of, :] = pre[mine, rows_of, :]
+        b_copies.append(exchange(
+            mine, chan, seq_count, lambda i: pre.at[i, rows_of], got_pre,
+            send_b, recv_b, part=part_of(b),
+        ))
+        if b == 0:
+            project(1)
     project(2)
     got_proj[mine] = proj_out[slot]
     p_copies = exchange(
         mine, chan, seq_count, lambda i: proj_out.at[lax.div(i, share)], got_proj, send_p, recv_p
     )
 
-    for copy in b_copies:
-        copy.wait()
-    for j in range(slots):
-        for r in range(base):
-            carried[r, j * per : (j + 1) * per, :] = got_pre[j * share, r * per : (r + 1) * per, :]
-
-    def convolve(h):
-        decay = [jnp.exp(-x) for x in params(0, h)]
-        weights = params(1, h)
-        direct = par[2 * modes * groups + 8 * h : 2 * modes * groups + 8 * h + 8, :]
-        for b in range(batch):
+    def convolve(b):
+        for copy in b_copies[b]:
+            copy.wait()
+        for j in range(slots):
+            for r in range(b * modes, (b + 1) * modes):
+                carried[r, j * per : (j + 1) * per, :] = got_pre[
+                    j * share, r * per : (r + 1) * per, :
+                ]
+        for h in range(groups // 8):
+            decay = [jnp.exp(-x) for x in params(0, h)]
+            weights = params(1, h)
+            direct = par[2 * modes * groups + 8 * h : 2 * modes * groups + 8 * h + 8, :]
 
             def step(t, state):
                 at = pl.ds(pl.multiple_of(t * groups + 8 * h, 8), 8)
@@ -220,9 +229,8 @@
             )
             lax.fori_loop(0, length, step, begin, unroll=4)
 
-    halves = groups // 8
-    for h in range(halves // 2):
-        convolve(h)
+    for b in range(batch - batch // 2):
+        convolve(b)
 
     for copy in p_copies:
         copy.wait()
@@ -255,8 +263,8 @@
     got_dec[mine] = dec[...]
     d_copies = exchange(mine, chan, seq_count, lambda i: dec, got_dec, send_d, recv_d)
 
-    for h in range(halves // 2, halves):
-        convolve(h)
+    for b in range(batch - batch // 2, batch):
+        convolve(b)
 
     for copy in d_copies:
         copy.wait()
@@ -292,7 +300,9 @@
     value = got_part[0]
     for c in range(1, chan_count):
         value = value + got_part[c]
-    decoded[...] = value.astype(BF16)
+    value = value.astype(BF16)
+    for b in range(batch):
+        decoded[b] = value[b * steps : (b + 1) * steps]
 
 
 def body(
@@ -321,7 +331,7 @@
         functools.partial(kernel, seq_count, chan_count),
         out_shape=(
             jax.ShapeDtypeStruct((batch, chans, length), BF16),
-            jax.ShapeDtypeStruct((count, piece), BF16),
+            jax.ShapeDtypeStruct((batch, steps, piece), BF16),
         ),
         in_specs=[ANY, SMEM, SMEM, ANY, ANY, ANY, ANY, ANY, ANY, ANY],
         out_specs=(VMEM, VMEM),
@@ -357,7 +367,11 @@
             sems(6),
             sems(5),
         ]
-        + [sems(seq_count - 1)] * 10
+        + [sems(seq_count - 1)] * 2
+        + [sems(batch * (seq_count - 1))] * 2
+        + [sems(seq_count - 1)] * 2
+        + [sems(batch * (seq_count - 1))] * 2
+        + [sems(seq_count - 1)] * 2
         + [sems(chan_count - 1)] * 2,
         compiler_params=pltpu.CompilerParams(
             vmem_limit_bytes=LIMIT, collective_id=0, has_side_effects=True
@@ -367,7 +381,7 @@
         features, offsets, tokens, decay_rate, residue, skip_weight[None],
         embedding, norm_gain[None], dec_weight, out_weight,
     )
-    return mixed, decoded.reshape(batch, steps, -1)
+    return mixed, decoded
 
 
 def solution(mesh):

time: 39.1 us -> 36.2 us (0.926)
  Pallas kernels: 34.7 us -> 31.8 us
    pallas_call x1, Pallas kernels: 34.7 us -> 31.8 us  [body(): pl.pallas_call(functools.partial(kernel, seq_count, chan_count), out_shap...]
    reshape x1 -> x0, local copies, waits for them, and re-layouts: 1.28 us -> none  [body(): return (mixed, decoded.reshape(batch, steps, -1))]
    unnamed x1 -> x2, local copies, waits for them, and re-layouts: 2.26 us -> 3.54 us
where the time goes in v4:
time: 36.2 us; the launch traced here: 36 us
  Pallas kernels  31.8 us (88%)
  local copies, waits for them, and re-layouts  3.54 us (10%)
  between operations  0.64 us (2%)
    pallas_call x1, Pallas kernels, body(): pl.pallas_call(functools.partial(kernel, seq_count, chan_count), out_shap...  31.8 us
    unnamed x2, local copies, waits for them, and re-layouts  3.54 us

profile of v4, /device:TPU:0, one launch (start us, length us, event | category | flops | bytes accessed | tf_op | source)
XLA Modules:
  0.0 36.0 jit_solution(10545778370264562767)
XLA Ops:
  0.6 31.8 %layer.1 = (bf16[2,2048,128]{2,1,0:T(8,128)(2,1)}, bf16[2,4,256]{2,1,0:T(4,128)(2,1)}) custom-call(bf16[3,2,2048,128]{3,2,1,0:T(8,128)(2,1)} %feat.1, s32[2]{0:T(128)} %offsets.1, s32[2,4]{1,0:T(2,128)} %tokens.1, f32[16,2048]{1,0:T(8,128)} %rate_hbm.1, f32[16,2048]{1,0:T(8,128)} %residue_hbm.1, f32[1,2048]{1,0:T(1,128)} %bitcast.2, ...), custom_call_target="tpu_custom_call" | custom-call | tf_op jit(solution)/shard_map/layer/pallas_call | solution.py:330
  32.4 2.3 %copy.14 = bf16[2,2048,128]{2,1,0:T(8,128)(2,1)} copy(bf16[2,2048,128]{2,1,0:T(8,128)(2,1)} %get-tuple-element.4) | data formatting | bytes 2097152
  34.7 1.3 %copy.15 = bf16[2,4,256]{2,1,0:T(4,128)(2,1)} copy(bf16[2,4,256]{2,1,0:T(4,128)(2,1)} %get-tuple-element.5) | data formatting | bytes 8192
